TPU v7x, 32 devices: a whole 2x2x4 slice. The times are simulated.
32 devices in a mesh: dp: 4 (over y, x), space: 8 (over z, core).
Axes of the slice: x: 2, y: 2, z: 4, core: 2. Of those that a mesh axis runs over, the one named last changes fastest.
Arguments:
- features: bfloat16 [4, 128, 128, 256], P('dp', 'space'), may hold values from -6 to 6
- heights: float32 [4, 128, 128], P('dp', 'space'), may hold values from 0.02 to 2
- cotangent: bfloat16 [4, 128, 128, 256], P('dp', 'space'), may hold values from -6 to 6
- weight_first: bfloat16 [3, 3, 256, 256], replicated, may hold values from -0.125 to 0.125
- weight_second: bfloat16 [3, 3, 256, 256], replicated, may hold values from -0.125 to 0.125
- shade_embed: bfloat16 [256], replicated, may hold values from -4 to 4
Outputs:
- grad_features: bfloat16 [4, 128, 128, 256], P('dp', 'space')
- grad_first: float32 [3, 3, 256, 256], replicated
- grad_second: float32 [3, 3, 256, 256], replicated
- grad_embed: float32 [256], replicated
All inputs are finite; a program needn't handle non-finite values.
Results may differ from a plain program's by a relative error of at most 0.012.
Values may be sent and summed in bfloat16 or wider, within the bound.
A program may use at most 64 MiB of HBM per device.

v0:
```python
import math
import jax
import jax.numpy as jnp
from jax import lax
from jax.sharding import PartitionSpec as P


def prefix(part, axis, combine, identity):
    place = lax.axis_index(axis)
    gathered = lax.all_gather(part, axis)
    state = jnp.zeros_like(part) + jnp.asarray(identity, part.dtype)

    def one(hop, state):
        return combine(state, lax.dynamic_index_in_dim(gathered, hop, 0, False))

    return lax.fori_loop(0, place, one, state)


def padded_2(cells, sides, width):
    for axis, dim in sides:
        count = lax.axis_size(axis)
        ends = count - 1
        head = lax.slice_in_dim(cells, 0, width, axis=dim)
        tail = lax.slice_in_dim(cells, cells.shape[dim] - width, cells.shape[dim], axis=dim)
        cells = jnp.concatenate(
            [
                lax.ppermute(tail, axis, [(i, (i + 1) % count) for i in range(ends)]),
                cells,
                lax.ppermute(head, axis, [((i + 1) % count, i) for i in range(ends)]),
            ],
            axis=dim,
        )
    return cells


def convolve(padded, kernel):
    return lax.conv_general_dilated(
        padded,
        kernel,
        (1, 1),
        ((0, 0), (1, 1)),
        dimension_numbers=("NHWC", "HWIO", "NHWC"),
        preferred_element_type=jnp.float32,
    )


def reversed_kernel(kernel):
    return jnp.transpose(jnp.flip(kernel, (0, 1)), (0, 1, 3, 2))


def silu_slope(values):
    sigma = jax.nn.sigmoid(values)
    return sigma * (1.0 + values * (1.0 - sigma))


def kernel_grad(padded, gradient):
    channels = gradient.shape[-1]
    row_count = gradient.shape[1]
    col_count = gradient.shape[2]
    widened = jnp.pad(padded, ((0, 0), (0, 0), (1, 1), (0, 0)))
    flat_grad = gradient.reshape(-1, channels)
    stacked = []
    for offset_row in range(3):
        line = []
        for offset_col in range(3):
            window = widened[
                :, offset_row : offset_row + row_count, offset_col : offset_col + col_count, :
            ].reshape(-1, channels)
            line.append(jnp.dot(window.T, flat_grad, preferred_element_type=jnp.float32))
        stacked.append(jnp.stack(line))
    return jnp.stack(stacked)


def body(features, heights, cotangent, weight_first, weight_second, shade_embed):
    images, strip, col_count, channels = features.shape
    space_count = lax.axis_size("space")
    total_rows = strip * space_count
    decline = 2.0 / total_rows
    strip_index = lax.axis_index("space")
    position = (strip_index * strip + jnp.arange(strip)).astype(jnp.float32)
    lifted = heights + decline * position[None, :, None]
    strip_peak = jnp.max(lifted, axis=1)
    carried = prefix(strip_peak, "space", jnp.maximum, jnp.zeros_like(strip_peak))
    running = lax.cummax(lifted, axis=1)
    earlier_max = jnp.concatenate(
        [carried[:, None, :], jnp.maximum(running[:, :-1, :], carried[:, None, :])], axis=1
    )
    shading = jnp.maximum(earlier_max - lifted, 0.0)
    mixed = (
        features.astype(jnp.float32) + shading[..., None] * shade_embed.astype(jnp.float32)
    ).astype(jnp.bfloat16)
    back_second = reversed_kernel(weight_second)
    back_first = reversed_kernel(weight_first)
    padded_in = padded_2(mixed, (("space", 1),), 1)
    hidden_pre = convolve(padded_in, weight_first)
    active = jax.nn.silu(hidden_pre).astype(jnp.bfloat16)
    active_pad = padded_2(active, (("space", 1),), 1)
    cot_pad = padded_2(cotangent, (("space", 1),), 1)
    back_act = convolve(cot_pad, back_second)
    back_hidden = (back_act * silu_slope(hidden_pre)).astype(jnp.bfloat16)
    hidden_pad = padded_2(back_hidden, (("space", 1),), 1)
    back_input = convolve(hidden_pad, back_first)
    grad_features = (cotangent.astype(jnp.float32) + back_input).astype(jnp.bfloat16)
    scaling = 1.0 / math.sqrt(images * lax.axis_size("dp") * total_rows * col_count)
    first_term = kernel_grad(padded_in, back_hidden).reshape(-1) * scaling
    second_term = kernel_grad(active_pad, cotangent).reshape(-1) * scaling
    embed_term = jnp.sum(shading[..., None] * back_input, axis=(0, 1, 2)) * scaling
    first_sum, second_sum, embed_sum = lax.psum(
        (first_term, second_term, embed_term), ("dp", "space")
    )
    kernel_shape = (3, 3, channels, channels)
    return (
        grad_features,
        first_sum.reshape(kernel_shape),
        second_sum.reshape(kernel_shape),
        embed_sum,
    )


def solution(mesh):
    in_specs = (
        P("dp", "space", None, None),
        P("dp", "space", None),
        P("dp", "space", None, None),
        P(),
        P(),
        P(),
    )
    out_specs = (P("dp", "space", None, None), P(), P(), P())
    return jax.shard_map(body, mesh=mesh, in_specs=in_specs, out_specs=out_specs, check_vma=False)
```

profile of v0, /device:TPU:0, one launch (start us, length us, event | category | flops | bytes accessed | tf_op | source)
XLA Modules:
  0.0 250.0 jit_solution(15768503703791382896)
XLA Ops:
  7.2 0.7 convert_element_type.34
  8.0 0.8 fusion.108
  8.8 13.4 %all-gather.1 = f32[8,1,128]{2,1,0:T(1,128)S(1)} all-gather(f32[1,1,128]{2,1,0:T(1,128)S(1)} %bitcast.222), channel_id=2, replica_groups=mesh['dp'=4,'space'=8] {'space'}, dimensions={0}, use_global_device_ids=true | all-gather | bytes 4608 | tf_op jit(solution)/shard_map/all_gather | solution.py:10
  22.1 1.7 copy.38
  24.3 2.2 collective-permute-start.2
  26.6 1.3 collective-permute-start.3
  27.9 0.7 fusion.111
  28.5 3.6 %collective-permute-start = (bf16[1,1,128,256]{3,2,1,0:T(8,128)(2,1)}, bf16[1,1,128,256]{3,2,1,0:T(8,128)(2,1)}, u32[]{:S(2)}, u32[]{:S(2)}) collective-permute-start(bf16[1,1,128,256]{3,2,1,0:T(8,128)(2,1)} %get-tuple-element.60), channel_id=1, source_target_pairs={{0,1},{1,2},{2,3},{3,4},{4,5},{5,6},{6,7},{8,9},{9,10},{10,11},{11... | collective-permute-start | bytes 196616 | tf_op jit(solution)/shard_map/ppermute | solution.py:27
  32.2 1.3 collective-permute-start.1
  33.5 1.2 pad_maximum_fusion
  34.7 1.4 copy.62
  36.1 1.7 pad.11.clone
  37.9 1.4 reshape.171
  39.3 1.8 copy.41
  41.2 4.4 %multiply_convert_fusion.1 = (bf16[16,8,17,256]{3,1,2,0:T(8,128)(2,1)S(1)}, f32[16,8,17,256]{3,1,2,0:T(8,128)}) fusion(pred[8,17]{0,1:T(8,128)(4,1)S(1)} %copy-done.27, bf16[3,3,256,256]{3,2,1,0:T(8,128)(2,1)S(1)} %copy-done, bf16[18,1,7,2,256]{4,2,3,0,1:T(8,128)(2,1)S(1)} %slice.130, bf16[18,1,8,17,256]{4,2,3,0,1:T(8,128)(2,1)S(1)} %copy.41), kind=kOutput, calls=%fused_computation.22 | convolution fusion | flops 2574458880 | bytes 5904520 | tf_op jit(solution)/shard_map/conv_general_dilated | solution.py:37
  45.5 0.6 fusion.109
  46.2 1.2 copy.52
  47.4 1.0 maximum_bitcast_fusion
  48.5 0.6 pad.9
  49.0 1.4 reshape.166
  50.5 1.9 copy.37
  52.4 4.7 %multiply_convert_fusion = bf16[16,8,17,256]{3,1,2,0:T(8,128)(2,1)S(1)} fusion(f32[16,8,17,256]{3,1,2,0:T(8,128)} %get-tuple-element.65, bf16[3,3,256,256]{3,2,1,0:T(8,128)(2,1)S(1)} %copy-done.26, bf16[18,1,7,2,256]{4,2,3,0,1:T(8,128)(2,1)S(1)} %slice.126, bf16[18,1,8,17,256]{4,2,3,0,1:T(8,128)(2,1)S(1)} %copy.37, pred[8,17]{0,1:T(8,128)(4,1)S(1)} %copy-done.27), kind=kOutput, calls=%fused_computation.21 | convolution fusion | flops 2577244160 | bytes 5904520 | tf_op jit(solution)/shard_map/conv_general_dilated | solution.py:37
  57.4 1.3 copy-done.3
  58.8 1.5 convolution_bitcast_fusion.13
  60.3 1.5 convolution_bitcast_fusion.17
  61.8 1.5 convolution_bitcast_fusion.9
  63.3 1.5 convolution_bitcast_fusion.11
  64.9 1.5 convolution_bitcast_fusion.12
  66.4 1.5 convolution_bitcast_fusion.14
  67.9 1.5 convolution_bitcast_fusion.15
  69.5 1.0 slice.140
  70.5 1.9 copy.60
  72.6 0.7 copy.59
  73.3 3.8 %collective-permute-start.6 = (bf16[1,1,128,256]{2,3,1,0:T(8,128)(2,1)}, bf16[1,1,128,256]{2,3,1,0:T(8,128)(2,1)}, u32[]{:S(2)}, u32[]{:S(2)}) collective-permute-start(bf16[1,1,128,256]{2,3,1,0:T(8,128)(2,1)} %copy.59), channel_id=1, source_target_pairs={{0,1},{1,2},{2,3},{3,4},{4,5},{5,6},{6,7},{8,9},{9,10},{10,11},{11... | collective-permute-start | bytes 196616 | tf_op jit(solution)/shard_map/ppermute | solution.py:27
  77.3 1.4 collective-permute-start.7
  79.3 0.8 convolution_bitcast_fusion.10
  80.4 0.8 convolution_bitcast_fusion.16
  81.6 1.6 maximum_multiply_fusion
  83.2 2.3 fusion.8
  85.6 0.4 convolution_bitcast_fusion.2
  86.0 0.5 convolution_bitcast_fusion.3
  87.0 0.5 convolution_bitcast_fusion.6
  88.0 0.5 convolution_bitcast_fusion
  89.0 1.3 convolution_bitcast_fusion.7
  90.4 1.6 maximum_multiply_fusion.1
  92.0 1.0 fusion.110
  93.1 0.6 slice.132
  93.8 3.7 %collective-permute-start.4 = (bf16[1,1,128,256]{3,2,1,0:T(8,128)(2,1)}, bf16[1,1,128,256]{3,2,1,0:T(8,128)(2,1)S(1)}, u32[]{:S(2)}, u32[]{:S(2)}) collective-permute-start(bf16[1,1,128,256]{3,2,1,0:T(8,128)(2,1)} %slice.132), channel_id=1, source_target_pairs={{0,1},{1,2},{2,3},{3,4},{4,5},{5,6},{6,7},{8,9},{9,10},{10,11},{11... | collective-permute-start | bytes 196616 | tf_op jit(solution)/shard_map/ppermute | solution.py:27
  97.5 0.6 slice.135
  98.1 1.3 collective-permute-start.5
  99.4 1.4 copy.35
  101.1 1.6 collective-permute-done.5
  102.9 1.7 pad.13
  104.5 2.3 reshape.188
  107.2 3.0 %convolution_select_fusion = f32[16,8,17,256]{3,1,2,0:T(8,128)S(1)} fusion(bf16[3,3,256,256]{3,2,1,0:T(8,128)(2,1)S(1)} %copy-done, bf16[18,1,7,2,256]{4,2,3,0,1:T(8,128)(2,1)S(1)} %slice.136, bf16[18,1,8,17,256]{4,2,3,0,1:T(8,128)(2,1)S(1)} %copy.47, pred[8,17]{0,1:T(8,128)(4,1)S(1)} %copy-done.27), kind=kOutput, calls=%fused_computation.29 | convolution fusion | flops 2571673600 | bytes 4790408 | tf_op jit(solution)/shard_map/conv_general_dilated | solution.py:37
  110.3 0.7 copy.48
  111.0 1.5 slice.137
  112.5 2.0 copy.58
  114.6 2.7 %fusion.9 = (f32[256]{0:T(256)S(1)}, bf16[1,16,128,256]{2,3,1,0:T(8,128)(2,1)}) fusion(f32[16,1,128,256]{2,3,0,1:T(8,128)S(1)} %copy.58, f32[16,128]{1,0:T(8,128)S(1)} %copy-done.21, bf16[1,16,128,256]{2,3,1,0:T(8,128)(2,1)} %copy.35), kind=kLoop, calls=%fused_computation.26 | loop fusion | flops 2621184 | bytes 4203520 | tf_op jit(solution)/shard_map/reduce_sum | solution.py:107
  117.2 2.3 copy.56
  119.5 42.8 %psum.23 = f32[256]{0:T(256)} all-reduce(f32[256]{0:T(256)S(1)} %broadcast_multiply_fusion), channel_id=1, replica_groups=mesh['dp'=4,'space'=8] {'dp','space'}, use_global_device_ids=true, to_apply=%region_7.8 | all-reduce | flops 256 | bytes 2048 | tf_op jit(solution)/shard_map/psum | solution.py:108
  162.3 76.1 %all-reduce.5.cloned.1.call-done = (f32[3,3,256,256]{3,2,1,0:T(8,128)}, f32[3,3,256,256]{3,2,1,0:T(8,128)}) async-done(((f32[3,3,256,256]{3,2,1,0:T(8,128)}, f32[3,3,256,256]{3,2,1,0:T(8,128)}), (f32[3,3,256,256]{3,2,1,0:T(8,128)}, f32[3,3,256,256]{3,2,1,0:T(8,128)})) %all-reduce.5.cloned.1.call-update) | async-done | bytes 4718608 | tf_op jit(solution)/shard_map/psum | solution.py:108
  238.4 3.4 %copy.109 = f32[3,3,256,256]{3,2,1,0:T(8,128)} copy(f32[3,3,256,256]{3,2,1,0:T(8,128)} %get-tuple-element.118) | data formatting | bytes 4718592
  241.7 1.4 copy.110
  (100 shorter events, 4.8 us)
Async XLA Ops:
  7.2 34.0 %copy-start = (bf16[3,3,256,256]{3,2,1,0:T(8,128)(2,1)S(1)}, bf16[3,3,256,256]{3,2,1,0:T(8,128)(2,1)}, u32[]{:S(2)}) copy-start(bf16[3,3,256,256]{3,2,1,0:T(8,128)(2,1)} %param.11) | copy-start | bytes 3538948
  7.2 231.2 %all-reduce.5.cloned.1.call-start = ((), (), s32[]{:S(2)}) async-start(), calls=%async_computation | async-start | bytes 9437184 | tf_op jit(solution)/shard_map/psum | solution.py:108
  22.1 5.7 %copy-start.1 = (bf16[1,16,128,256]{3,2,1,0:T(8,128)(2,1)S(1)}, bf16[1,16,128,256]{3,2,1,0:T(8,128)(2,1)}, u32[]{:S(2)}) copy-start(bf16[1,16,128,256]{3,2,1,0:T(8,128)(2,1)} %param.10) | copy-start | bytes 3145732
  23.9 9.6 %copy-start.20 = (f32[16,128]{1,0:T(8,128)}, f32[16,128]{1,0:T(8,128)S(1)}, u32[]{:S(2)}) copy-start(f32[16,128]{1,0:T(8,128)S(1)} %fusion.78) | copy-start | bytes 24580
  24.3 9.2 %copy-start.2 = (bf16[1,16,128,256]{2,3,1,0:T(8,128)(2,1)}, bf16[1,16,128,256]{2,3,1,0:T(8,128)(2,1)S(1)}, u32[]{:S(2)}) copy-start(bf16[1,16,128,256]{2,3,1,0:T(8,128)(2,1)S(1)} %add_convert_fusion) | copy-start | bytes 3145732
  24.3 9.1 %collective-permute-start.2 = (bf16[1,1,128,256]{2,3,1,0:T(8,128)(2,1)S(1)}, bf16[1,1,128,256]{2,3,1,0:T(8,128)(2,1)S(1)}, u32[]{:S(2)}, u32[]{:S(2)}) collective-permute-start(bf16[1,1,128,256]{2,3,1,0:T(8,128)(2,1)S(1)} %get-tuple-element.62), channel_id=1, source_target_pairs={{0,1},{1,2},{2,3},{3,4},{4,5},{5,6},{6,7},{8,9},{9,10},{10,11},{11... | collective-permute-start | bytes 196616 | tf_op jit(solution)/shard_map/ppermute | solution.py:27
  26.6 6.9 %collective-permute-start.3 = (bf16[1,1,128,256]{2,3,1,0:T(8,128)(2,1)S(1)}, bf16[1,1,128,256]{2,3,1,0:T(8,128)(2,1)S(1)}, u32[]{:S(2)}, u32[]{:S(2)}) collective-permute-start(bf16[1,1,128,256]{2,3,1,0:T(8,128)(2,1)S(1)} %get-tuple-element.63), channel_id=1, source_target_pairs={{1,0},{2,1},{3,2},{4,3},{5,4},{6,5},{7,6},{9,8},{10,9},{11,10},{12... | collective-permute-start | bytes 196616 | tf_op jit(solution)/shard_map/ppermute | solution.py:29
  28.5 18.9 %collective-permute-start = (bf16[1,1,128,256]{3,2,1,0:T(8,128)(2,1)}, bf16[1,1,128,256]{3,2,1,0:T(8,128)(2,1)}, u32[]{:S(2)}, u32[]{:S(2)}) collective-permute-start(bf16[1,1,128,256]{3,2,1,0:T(8,128)(2,1)} %get-tuple-element.60), channel_id=1, source_target_pairs={{0,1},{1,2},{2,3},{3,4},{4,5},{5,6},{6,7},{8,9},{9,10},{10,11},{11... | collective-permute-start | bytes 196616 | tf_op jit(solution)/shard_map/ppermute | solution.py:27
  32.2 15.3 %collective-permute-start.1 = (bf16[1,1,128,256]{3,2,1,0:T(8,128)(2,1)}, bf16[1,1,128,256]{3,2,1,0:T(8,128)(2,1)}, u32[]{:S(2)}, u32[]{:S(2)}) collective-permute-start(bf16[1,1,128,256]{3,2,1,0:T(8,128)(2,1)} %get-tuple-element.61), channel_id=1, source_target_pairs={{1,0},{2,1},{3,2},{4,3},{5,4},{6,5},{7,6},{9,8},{10,9},{11,10},{12... | collective-permute-start | bytes 196616 | tf_op jit(solution)/shard_map/ppermute | solution.py:29
  33.5 1.3 copy-start.22
  33.5 1.2 copy-start.24
  39.3 1.9 copy-start.27
  50.5 1.9 copy-start.26
  57.1 3.1 %copy-start.10 = (bf16[16,8,17,256]{3,1,2,0:T(8,128)(2,1)}, bf16[16,8,17,256]{3,1,2,0:T(8,128)(2,1)S(1)}, u32[]{:S(2)}) copy-start(bf16[16,8,17,256]{3,1,2,0:T(8,128)(2,1)S(1)} %multiply_convert_fusion) | copy-start | bytes 3342340
  57.1 1.6 copy-start.3
  57.4 2.9 %copy-start.11 = (bf16[1,18,128,256]{2,3,1,0:T(8,128)(2,1)S(1)}, bf16[1,18,128,256]{2,3,1,0:T(8,128)(2,1)}, u32[]{:S(2)}) copy-start(bf16[1,18,128,256]{2,3,1,0:T(8,128)(2,1)} %get-tuple-element.54) | copy-start | bytes 3538948
  58.8 9.2 %copy-start.6 = (bf16[16,1,128,256]{3,0,2,1:T(8,128)(2,1)}, bf16[16,1,128,256]{3,0,2,1:T(8,128)(2,1)S(1)}, u32[]{:S(2)}) copy-start(bf16[16,1,128,256]{3,0,2,1:T(8,128)(2,1)S(1)} %slice.133) | copy-start | bytes 3145732
  67.9 1.6 copy-start.5
  69.5 3.0 %copy-start.12 = (bf16[1,8,17,256]{3,1,2,0:T(8,128)(2,1)S(1)}, bf16[1,8,17,256]{3,1,2,0:T(8,128)(2,1)}, u32[]{:S(2)}) copy-start(bf16[1,8,17,256]{3,1,2,0:T(8,128)(2,1)} %get-tuple-element.56) | copy-start | bytes 208900
  73.3 9.9 %collective-permute-start.6 = (bf16[1,1,128,256]{2,3,1,0:T(8,128)(2,1)}, bf16[1,1,128,256]{2,3,1,0:T(8,128)(2,1)}, u32[]{:S(2)}, u32[]{:S(2)}) collective-permute-start(bf16[1,1,128,256]{2,3,1,0:T(8,128)(2,1)} %copy.59), channel_id=1, source_target_pairs={{0,1},{1,2},{2,3},{3,4},{4,5},{5,6},{6,7},{8,9},{9,10},{10,11},{11... | collective-permute-start | bytes 196616 | tf_op jit(solution)/shard_map/ppermute | solution.py:27
  77.1 2.1 copy-start.25
  77.3 1.9 copy-start.4
  77.3 1.9 copy-start.7
  77.3 5.9 %collective-permute-start.7 = (bf16[1,1,128,256]{2,3,1,0:T(8,128)(2,1)S(1)}, bf16[1,1,128,256]{2,3,1,0:T(8,128)(2,1)S(1)}, u32[]{:S(2)}, u32[]{:S(2)}) collective-permute-start(bf16[1,1,128,256]{2,3,1,0:T(8,128)(2,1)S(1)} %copy.61), channel_id=1, source_target_pairs={{1,0},{2,1},{3,2},{4,3},{5,4},{6,5},{7,6},{9,8},{10,9},{11,10},{12... | collective-permute-start | bytes 196616 | tf_op jit(solution)/shard_map/ppermute | solution.py:29
  79.2 1.0 copy-start.18
  79.2 1.0 copy-start.19
  79.2 1.1 copy-start.23
  80.3 0.9 copy-start.13
  80.3 1.0 copy-start.14
  80.3 1.1 copy-start.15
  80.3 1.2 copy-start.16
  80.3 1.3 copy-start.17
  92.0 8.7 %copy-start.8 = (bf16[16,1,128,256]{3,0,2,1:T(8,128)(2,1)S(1)}, bf16[16,1,128,256]{3,0,2,1:T(8,128)(2,1)}, u32[]{:S(2)}) copy-start(bf16[16,1,128,256]{3,0,2,1:T(8,128)(2,1)} %copy-done.6) | copy-start | bytes 3145732
  93.8 7.4 %collective-permute-start.4 = (bf16[1,1,128,256]{3,2,1,0:T(8,128)(2,1)}, bf16[1,1,128,256]{3,2,1,0:T(8,128)(2,1)S(1)}, u32[]{:S(2)}, u32[]{:S(2)}) collective-permute-start(bf16[1,1,128,256]{3,2,1,0:T(8,128)(2,1)} %slice.132), channel_id=1, source_target_pairs={{0,1},{1,2},{2,3},{3,4},{4,5},{5,6},{6,7},{8,9},{9,10},{10,11},{11... | collective-permute-start | bytes 196616 | tf_op jit(solution)/shard_map/ppermute | solution.py:27
  98.1 4.6 %collective-permute-start.5 = (bf16[1,1,128,256]{3,2,1,0:T(8,128)(2,1)}, bf16[1,1,128,256]{3,2,1,0:T(8,128)(2,1)S(1)}, u32[]{:S(2)}, u32[]{:S(2)}) collective-permute-start(bf16[1,1,128,256]{3,2,1,0:T(8,128)(2,1)} %slice.135), channel_id=1, source_target_pairs={{1,0},{2,1},{3,2},{4,3},{5,4},{6,5},{7,6},{9,8},{10,9},{11,10},{12... | collective-permute-start | bytes 196616 | tf_op jit(solution)/shard_map/ppermute | solution.py:29
  112.5 2.0 copy-start.21
  238.4 3.4 %copy-start.9 = (f32[3,3,256,256]{3,2,1,0:T(8,128)S(1)}, f32[3,3,256,256]{3,2,1,0:T(8,128)}, u32[]{:S(2)}) copy-start(f32[3,3,256,256]{3,2,1,0:T(8,128)} %get-tuple-element.119) | copy-start | bytes 7077892
Sparse Core Ops, SparseCore 0:
  92.2 146.1 all-reduce.4
where the time goes:
time: 251 us; the launch traced here: 250 us
  waiting for transfers between devices  77.7 us (31%)
  blocking collectives  56.1 us (22%)
  local copies, waits for them, and re-layouts  40.5 us (16%)
  matrix products  29.5 us (12%)
  starting transfers between devices  18.6 us (7%)
  between operations  14.7 us (6%)
  other arithmetic  12.8 us (5%)
    psum x1, waiting for transfers between devices, body(): lax.psum((first_term, second_term, embed_term), ('dp', 'space'))  76.1 us
    psum x1, blocking collectives, body(): lax.psum((first_term, second_term, embed_term), ('dp', 'space'))  42.8 us
    unnamed x67, local copies, waits for them, and re-layouts  18.6 us
    dot_general x18, matrix products, kernel_grad(): jnp.dot(window.T, flat_grad, preferred_element_type=jnp.float32)  17.4 us
    all_gather x1, blocking collectives, prefix(): gathered = lax.all_gather(part, axis)  13.4 us
    ppermute x4, starting transfers between devices, padded_2(): lax.ppermute(tail, axis, [(i, (i + 1) % count) for i in range(ends)])  13.3 us
    conv_general_dilated x3, matrix products, convolve(): lax.conv_general_dilated(padded, kernel, (1, 1), ((0, 0), (1, 1)), dimens...  12.1 us
    conv_general_dilated x11, local copies, waits for them, and re-layouts, convolve(): lax.conv_general_dilated(padded, kernel, (1, 1), ((0, 0), (1, 1)), dimens...  11.5 us
  transfers between devices with their start and end apart: 9, of which 2 were waited for; matrix products, arithmetic and copies ran while one was open for 16% of the time, Pallas kernels for 0%

commit v1 on v0

--- a/solution.py
+++ b/solution.py
@@ -106,7 +106,7 @@
     second_term = kernel_grad(active_pad, cotangent).reshape(-1) * scaling
     embed_term = jnp.sum(shading[..., None] * back_input, axis=(0, 1, 2)) * scaling
     first_sum, second_sum, embed_sum = lax.psum(
-        (first_term, second_term, embed_term), ("dp", "space")
+        lax.psum((first_term, second_term, embed_term), axis_name="space"), axis_name="dp"
     )
     kernel_shape = (3, 3, channels, channels)
     return (

time: 251 us -> 335 us (1.33)
  waiting for transfers between devices: 77.7 us -> 169 us
  blocking collectives: 56.1 us -> 40.9 us
  local copies, waits for them, and re-layouts: 40.5 us -> 53 us
    psum x1 -> x2, waiting for transfers between devices: 76.1 us -> 168 us  [the longest x1 108 us: body(): lax.psum((first_term, second_term, embed_term), axis_name='space')]
    psum x1 -> x2, blocking collectives: 42.8 us -> 27.5 us  [the longest x1 16.8 us: body(): lax.psum((first_term, second_term, embed_term), axis_name='space')]
    reshape x0 -> x2, local copies, waits for them, and re-layouts: none -> 6.96 us  [the longest x1 3.48 us: body(): first_sum.reshape(kernel_shape)]
    unnamed x67 -> x69, local copies, waits for them, and re-layouts: 18.6 us -> 24.2 us
  transfers between devices with their start and end apart: 9 -> 10, of which waited for: 2 -> 3; matrix products, arithmetic and copies ran while one was open for 16% -> 12% of each run, Pallas kernels for 0% -> 0%
where the time goes in v1:
time: 335 us; the launch traced here: 334 us
  waiting for transfers between devices  169 us (50%)
  local copies, waits for them, and re-layouts  53 us (16%)
  blocking collectives  40.9 us (12%)
  matrix products  29.5 us (9%)
  starting transfers between devices  16.7 us (5%)
  between operations  14.7 us (4%)
  other arithmetic  9.97 us (3%)
    psum x1, waiting for transfers between devices, body(): lax.psum((first_term, second_term, embed_term), axis_name='space')  108 us
    psum x1, waiting for transfers between devices, body(): lax.psum(lax.psum((first_term, second_term, embed_term), axis_name='space...  60.1 us
    unnamed x69, local copies, waits for them, and re-layouts  24.2 us
    dot_general x18, matrix products, kernel_grad(): jnp.dot(window.T, flat_grad, preferred_element_type=jnp.float32)  17.4 us
    psum x1, blocking collectives, body(): lax.psum((first_term, second_term, embed_term), axis_name='space')  16.8 us
    all_gather x1, blocking collectives, prefix(): gathered = lax.all_gather(part, axis)  13.4 us
    conv_general_dilated x3, matrix products, convolve(): lax.conv_general_dilated(padded, kernel, (1, 1), ((0, 0), (1, 1)), dimens...  12.1 us
    conv_general_dilated x11, local copies, waits for them, and re-layouts, convolve(): lax.conv_general_dilated(padded, kernel, (1, 1), ((0, 0), (1, 1)), dimens...  11.6 us
  transfers between devices with their start and end apart: 10, of which 3 were waited for; matrix products, arithmetic and copies ran while one was open for 12% of the time, Pallas kernels for 0%

profile of v1, /device:TPU:0, one launch (start us, length us, event | category | flops | bytes accessed | tf_op | source)
XLA Modules:
  0.0 334.3 jit_solution(11482023445694179087)
XLA Ops:
  7.2 0.7 convert_element_type.34
  8.0 0.8 fusion.108
  8.8 13.4 %all-gather.1 = f32[8,1,128]{2,1,0:T(1,128)S(1)} all-gather(f32[1,1,128]{2,1,0:T(1,128)S(1)} %bitcast.230), channel_id=2, replica_groups=mesh['dp'=4,'space'=8] {'space'}, dimensions={0}, use_global_device_ids=true | all-gather | bytes 4608 | tf_op jit(solution)/shard_map/all_gather | solution.py:10
  22.1 1.7 copy.38
  24.3 2.2 collective-permute-start.2
  26.6 1.3 collective-permute-start.3
  27.9 0.7 fusion.111
  28.5 3.6 %collective-permute-start = (bf16[1,1,128,256]{3,2,1,0:T(8,128)(2,1)}, bf16[1,1,128,256]{3,2,1,0:T(8,128)(2,1)}, u32[]{:S(2)}, u32[]{:S(2)}) collective-permute-start(bf16[1,1,128,256]{3,2,1,0:T(8,128)(2,1)} %get-tuple-element.62), channel_id=1, source_target_pairs={{0,1},{1,2},{2,3},{3,4},{4,5},{5,6},{6,7},{8,9},{9,10},{10,11},{11... | collective-permute-start | bytes 196616 | tf_op jit(solution)/shard_map/ppermute | solution.py:27
  32.2 1.3 collective-permute-start.1
  33.5 1.2 pad_maximum_fusion
  34.7 1.4 copy.62
  36.1 1.7 pad.11.clone
  37.9 1.4 reshape.169
  39.3 1.8 copy.41
  41.2 4.4 %multiply_convert_fusion.1 = (bf16[16,8,17,256]{3,1,2,0:T(8,128)(2,1)S(1)}, f32[16,8,17,256]{3,1,2,0:T(8,128)}) fusion(pred[8,17]{0,1:T(8,128)(4,1)S(1)} %copy-done.27, bf16[3,3,256,256]{3,2,1,0:T(8,128)(2,1)S(1)} %copy-done, bf16[18,1,7,2,256]{4,2,3,0,1:T(8,128)(2,1)S(1)} %slice.130, bf16[18,1,8,17,256]{4,2,3,0,1:T(8,128)(2,1)S(1)} %copy.41), kind=kOutput, calls=%fused_computation.22 | convolution fusion | flops 2574458880 | bytes 5904520 | tf_op jit(solution)/shard_map/conv_general_dilated | solution.py:37
  45.5 0.6 fusion.109
  46.2 1.2 copy.52
  47.4 1.0 maximum_bitcast_fusion
  48.4 0.6 pad.9
  49.0 1.4 reshape.164
  50.4 1.9 copy.37
  52.4 4.7 %multiply_convert_fusion = bf16[16,8,17,256]{3,1,2,0:T(8,128)(2,1)S(1)} fusion(f32[16,8,17,256]{3,1,2,0:T(8,128)} %get-tuple-element.67, bf16[3,3,256,256]{3,2,1,0:T(8,128)(2,1)S(1)} %copy-done.26, bf16[18,1,7,2,256]{4,2,3,0,1:T(8,128)(2,1)S(1)} %slice.126, bf16[18,1,8,17,256]{4,2,3,0,1:T(8,128)(2,1)S(1)} %copy.37, pred[8,17]{0,1:T(8,128)(4,1)S(1)} %copy-done.27), kind=kOutput, calls=%fused_computation.21 | convolution fusion | flops 2577244160 | bytes 5904520 | tf_op jit(solution)/shard_map/conv_general_dilated | solution.py:37
  57.4 1.3 copy-done.3
  58.7 1.5 convolution_bitcast_fusion.13
  60.3 1.5 convolution_bitcast_fusion.17
  61.8 1.5 convolution_bitcast_fusion.9
  63.3 1.5 convolution_bitcast_fusion.11
  64.9 1.5 convolution_bitcast_fusion.12
  66.4 1.5 convolution_bitcast_fusion.14
  68.0 1.5 convolution_bitcast_fusion.15
  69.5 1.0 slice.140
  70.5 1.9 copy.60
  72.6 0.7 copy.59
  73.3 3.8 %collective-permute-start.6 = (bf16[1,1,128,256]{2,3,1,0:T(8,128)(2,1)}, bf16[1,1,128,256]{2,3,1,0:T(8,128)(2,1)}, u32[]{:S(2)}, u32[]{:S(2)}) collective-permute-start(bf16[1,1,128,256]{2,3,1,0:T(8,128)(2,1)} %copy.59), channel_id=1, source_target_pairs={{0,1},{1,2},{2,3},{3,4},{4,5},{5,6},{6,7},{8,9},{9,10},{10,11},{11... | collective-permute-start | bytes 196616 | tf_op jit(solution)/shard_map/ppermute | solution.py:27
  77.3 1.4 collective-permute-start.7
  79.3 0.8 convolution_bitcast_fusion.10
  80.4 0.8 convolution_bitcast_fusion.16
  81.8 2.6 copy.63
  84.5 2.3 fusion.8
  90.3 1.3 convolution_bitcast_fusion.7
  91.8 2.6 copy.64
  94.5 107.9 %all-reduce.7.cloned.1.call-done = (f32[589824]{0:T(1024)}, f32[589824]{0:T(1024)}) async-done(((f32[589824]{0:T(1024)}, f32[589824]{0:T(1024)}), (f32[589824]{0:T(1024)}, f32[589824]{0:T(1024)})) %all-reduce.7.cloned.1.call-update) | async-done | bytes 4718608 | tf_op jit(solution)/shard_map/psum | solution.py:109
  202.4 3.5 %reshape.150 = f32[3,3,256,256]{3,2,1,0:T(8,128)} reshape(f32[589824]{0:T(1024)} %get-tuple-element.48) | data formatting | bytes 4718592 | tf_op jit(solution)/shard_map/reshape | solution.py:114
  205.9 3.5 %reshape.161 = f32[3,3,256,256]{3,2,1,0:T(8,128)} reshape(f32[589824]{0:T(1024)} %get-tuple-element.49) | data formatting | bytes 4718592 | tf_op jit(solution)/shard_map/reshape | solution.py:115
  209.4 1.0 fusion.110
  210.5 0.6 slice.132
  211.2 1.7 collective-permute-start.4
  212.9 0.6 slice.135
  213.5 1.3 collective-permute-start.5
  214.8 1.6 copy.35
  216.8 1.4 collective-permute-done.5
  218.4 1.6 pad.13
  220.0 2.3 reshape.186
  222.7 3.0 convolution_select_fusion
  225.8 0.7 copy.48
  226.5 1.5 slice.137
  228.0 2.1 copy.58
  230.2 2.6 fusion.9
  232.8 2.3 copy.56
  235.1 16.8 %psum.46 = f32[256]{0:T(256)S(1)} all-reduce(f32[256]{0:T(256)S(1)} %broadcast_multiply_fusion), channel_id=1, replica_groups=mesh['dp'=4,'space'=8] {'space'}, use_global_device_ids=true, to_apply=%region_9.10 | all-reduce | flops 256 | bytes 2048 | tf_op jit(solution)/shard_map/psum | solution.py:109
  251.9 10.7 %psum.47 = f32[256]{0:T(256)} all-reduce(f32[256]{0:T(256)S(1)} %psum.46), channel_id=1, replica_groups=mesh['dp'=4,'space'=8] {'dp'}, use_global_device_ids=true, to_apply=%region_10.11 | all-reduce | flops 256 | bytes 2048 | tf_op jit(solution)/shard_map/psum | solution.py:108
  262.6 60.1 %all-reduce.9.cloned.1.call-done = (f32[3,3,256,256]{3,2,1,0:T(8,128)}, f32[3,3,256,256]{3,2,1,0:T(8,128)}) async-done(((f32[3,3,256,256]{3,2,1,0:T(8,128)}, f32[3,3,256,256]{3,2,1,0:T(8,128)}), (f32[3,3,256,256]{3,2,1,0:T(8,128)}, f32[3,3,256,256]{3,2,1,0:T(8,128)})) %all-reduce.9.cloned.1.call-update) | async-done | bytes 4718608 | tf_op jit(solution)/shard_map/psum | solution.py:108
  322.6 3.4 %copy.113 = f32[3,3,256,256]{3,2,1,0:T(8,128)} copy(f32[3,3,256,256]{3,2,1,0:T(8,128)} %get-tuple-element.120) | data formatting | bytes 4718592
  326.0 1.4 copy.114
  (108 shorter events, 7.2 us)
Async XLA Ops:
  7.2 34.0 %copy-start = (bf16[3,3,256,256]{3,2,1,0:T(8,128)(2,1)S(1)}, bf16[3,3,256,256]{3,2,1,0:T(8,128)(2,1)}, u32[]{:S(2)}) copy-start(bf16[3,3,256,256]{3,2,1,0:T(8,128)(2,1)} %param.11) | copy-start | bytes 3538948
  7.2 195.3 %all-reduce.7.cloned.1.call-start = ((), (), s32[]{:S(2)}) async-start(), calls=%async_computation | async-start | bytes 9437184 | tf_op jit(solution)/shard_map/psum | solution.py:109
  22.1 5.7 %copy-start.1 = (bf16[1,16,128,256]{3,2,1,0:T(8,128)(2,1)S(1)}, bf16[1,16,128,256]{3,2,1,0:T(8,128)(2,1)}, u32[]{:S(2)}) copy-start(bf16[1,16,128,256]{3,2,1,0:T(8,128)(2,1)} %param.10) | copy-start | bytes 3145732
  23.9 9.6 %copy-start.20 = (f32[16,128]{1,0:T(8,128)}, f32[16,128]{1,0:T(8,128)S(1)}, u32[]{:S(2)}) copy-start(f32[16,128]{1,0:T(8,128)S(1)} %fusion.78) | copy-start | bytes 24580
  24.3 9.2 %copy-start.2 = (bf16[1,16,128,256]{2,3,1,0:T(8,128)(2,1)}, bf16[1,16,128,256]{2,3,1,0:T(8,128)(2,1)S(1)}, u32[]{:S(2)}) copy-start(bf16[1,16,128,256]{2,3,1,0:T(8,128)(2,1)S(1)} %add_convert_fusion) | copy-start | bytes 3145732
  24.3 9.1 %collective-permute-start.2 = (bf16[1,1,128,256]{2,3,1,0:T(8,128)(2,1)S(1)}, bf16[1,1,128,256]{2,3,1,0:T(8,128)(2,1)S(1)}, u32[]{:S(2)}, u32[]{:S(2)}) collective-permute-start(bf16[1,1,128,256]{2,3,1,0:T(8,128)(2,1)S(1)} %get-tuple-element.64), channel_id=1, source_target_pairs={{0,1},{1,2},{2,3},{3,4},{4,5},{5,6},{6,7},{8,9},{9,10},{10,11},{11... | collective-permute-start | bytes 196616 | tf_op jit(solution)/shard_map/ppermute | solution.py:27
  26.6 6.9 %collective-permute-start.3 = (bf16[1,1,128,256]{2,3,1,0:T(8,128)(2,1)S(1)}, bf16[1,1,128,256]{2,3,1,0:T(8,128)(2,1)S(1)}, u32[]{:S(2)}, u32[]{:S(2)}) collective-permute-start(bf16[1,1,128,256]{2,3,1,0:T(8,128)(2,1)S(1)} %get-tuple-element.65), channel_id=1, source_target_pairs={{1,0},{2,1},{3,2},{4,3},{5,4},{6,5},{7,6},{9,8},{10,9},{11,10},{12... | collective-permute-start | bytes 196616 | tf_op jit(solution)/shard_map/ppermute | solution.py:29
  28.5 18.9 %collective-permute-start = (bf16[1,1,128,256]{3,2,1,0:T(8,128)(2,1)}, bf16[1,1,128,256]{3,2,1,0:T(8,128)(2,1)}, u32[]{:S(2)}, u32[]{:S(2)}) collective-permute-start(bf16[1,1,128,256]{3,2,1,0:T(8,128)(2,1)} %get-tuple-element.62), channel_id=1, source_target_pairs={{0,1},{1,2},{2,3},{3,4},{4,5},{5,6},{6,7},{8,9},{9,10},{10,11},{11... | collective-permute-start | bytes 196616 | tf_op jit(solution)/shard_map/ppermute | solution.py:27
  32.2 15.2 %collective-permute-start.1 = (bf16[1,1,128,256]{3,2,1,0:T(8,128)(2,1)}, bf16[1,1,128,256]{3,2,1,0:T(8,128)(2,1)}, u32[]{:S(2)}, u32[]{:S(2)}) collective-permute-start(bf16[1,1,128,256]{3,2,1,0:T(8,128)(2,1)} %get-tuple-element.63), channel_id=1, source_target_pairs={{1,0},{2,1},{3,2},{4,3},{5,4},{6,5},{7,6},{9,8},{10,9},{11,10},{12... | collective-permute-start | bytes 196616 | tf_op jit(solution)/shard_map/ppermute | solution.py:29
  33.5 1.2 copy-start.22
  33.5 1.2 copy-start.24
  39.3 1.9 copy-start.27
  50.4 1.9 copy-start.26
  57.1 3.1 copy-start.10
  57.1 1.6 copy-start.3
  57.4 2.9 copy-start.11
  58.7 9.2 %copy-start.6 = (bf16[16,1,128,256]{3,0,2,1:T(8,128)(2,1)}, bf16[16,1,128,256]{3,0,2,1:T(8,128)(2,1)S(1)}, u32[]{:S(2)}) copy-start(bf16[16,1,128,256]{3,0,2,1:T(8,128)(2,1)S(1)} %slice.133) | copy-start | bytes 3145732
  68.0 1.5 copy-start.5
  69.5 3.0 copy-start.12
  73.3 11.2 %collective-permute-start.6 = (bf16[1,1,128,256]{2,3,1,0:T(8,128)(2,1)}, bf16[1,1,128,256]{2,3,1,0:T(8,128)(2,1)}, u32[]{:S(2)}, u32[]{:S(2)}) collective-permute-start(bf16[1,1,128,256]{2,3,1,0:T(8,128)(2,1)} %copy.59), channel_id=1, source_target_pairs={{0,1},{1,2},{2,3},{3,4},{4,5},{5,6},{6,7},{8,9},{9,10},{10,11},{11... | collective-permute-start | bytes 196616 | tf_op jit(solution)/shard_map/ppermute | solution.py:27
  77.1 2.1 copy-start.25
  77.3 1.9 copy-start.4
  77.3 1.9 copy-start.7
  77.3 7.1 %collective-permute-start.7 = (bf16[1,1,128,256]{2,3,1,0:T(8,128)(2,1)S(1)}, bf16[1,1,128,256]{2,3,1,0:T(8,128)(2,1)S(1)}, u32[]{:S(2)}, u32[]{:S(2)}) collective-permute-start(bf16[1,1,128,256]{2,3,1,0:T(8,128)(2,1)S(1)} %copy.61), channel_id=1, source_target_pairs={{1,0},{2,1},{3,2},{4,3},{5,4},{6,5},{7,6},{9,8},{10,9},{11,10},{12... | collective-permute-start | bytes 196616 | tf_op jit(solution)/shard_map/ppermute | solution.py:29
  79.2 1.0 copy-start.18
  79.3 1.0 copy-start.19
  79.3 1.1 copy-start.23
  80.3 0.9 copy-start.13
  80.3 1.0 copy-start.14
  80.3 1.1 copy-start.15
  80.3 1.2 copy-start.16
  80.3 1.3 copy-start.17
  94.5 228.2 %all-reduce.9.cloned.1.call-start = ((), (), s32[]{:S(2)}) async-start(), calls=%async_computation.1 | async-start | bytes 9437184 | tf_op jit(solution)/shard_map/psum | solution.py:108
  209.4 7.0 %copy-start.8 = (bf16[16,1,128,256]{3,0,2,1:T(8,128)(2,1)S(1)}, bf16[16,1,128,256]{3,0,2,1:T(8,128)(2,1)}, u32[]{:S(2)}) copy-start(bf16[16,1,128,256]{3,0,2,1:T(8,128)(2,1)} %copy-done.6) | copy-start | bytes 3145732
  211.2 5.6 %collective-permute-start.4 = (bf16[1,1,128,256]{3,2,1,0:T(8,128)(2,1)}, bf16[1,1,128,256]{3,2,1,0:T(8,128)(2,1)S(1)}, u32[]{:S(2)}, u32[]{:S(2)}) collective-permute-start(bf16[1,1,128,256]{3,2,1,0:T(8,128)(2,1)} %slice.132), channel_id=1, source_target_pairs={{0,1},{1,2},{2,3},{3,4},{4,5},{5,6},{6,7},{8,9},{9,10},{10,11},{11... | collective-permute-start | bytes 196616 | tf_op jit(solution)/shard_map/ppermute | solution.py:27
  213.5 4.7 %collective-permute-start.5 = (bf16[1,1,128,256]{3,2,1,0:T(8,128)(2,1)}, bf16[1,1,128,256]{3,2,1,0:T(8,128)(2,1)S(1)}, u32[]{:S(2)}, u32[]{:S(2)}) collective-permute-start(bf16[1,1,128,256]{3,2,1,0:T(8,128)(2,1)} %slice.135), channel_id=1, source_target_pairs={{1,0},{2,1},{3,2},{4,3},{5,4},{6,5},{7,6},{9,8},{10,9},{11,10},{12... | collective-permute-start | bytes 196616 | tf_op jit(solution)/shard_map/ppermute | solution.py:29
  228.0 2.1 copy-start.21
  322.6 3.4 %copy-start.9 = (f32[3,3,256,256]{3,2,1,0:T(8,128)S(1)}, f32[3,3,256,256]{3,2,1,0:T(8,128)}, u32[]{:S(2)}) copy-start(f32[3,3,256,256]{3,2,1,0:T(8,128)} %get-tuple-element.121) | copy-start | bytes 7077892
Sparse Core Ops, SparseCore 0:
  94.6 107.7 all-reduce.6
  209.5 113.0 all-reduce.8
